TPU v7x, 32 devices: a whole 2x2x4 slice. The times are simulated.
32 devices in a mesh: runs: 2 (over x), space: 16 (over z, y, core).
Axes of the slice: x: 2, y: 2, z: 4, core: 2. Of those that a mesh axis runs over, the one named last changes fastest.
Arguments:
- fields: float32 [128, 512], P(('runs', 'space')), parts along dimension 0, may hold values from -3 to 3
- end_weights: bfloat16 [256, 128, 512], P(None, ('runs', 'space')), parts along dimension 1, may hold values from 0.5 to 1.5
- directions: float32 [3, 256], replicated, may hold values from -1 to 1
- analysis: bfloat16 [256, 256], replicated, may hold values from -0.375 to 0.375
- synthesis: bfloat16 [256, 256], replicated, may hold values from -0.375 to 0.375
- decay_rates: float32 [256], replicated, may hold values from 0.1 to 1
Outputs:
- density: float32 [128, 512], P(('runs', 'space')), parts along dimension 0
There are 2 independent parts, one for each index of `runs`. A program takes and returns all parts, laid end to end along the dimension named above; an argument that names none is the same for every part. Nothing has to cross between parts.
All inputs are finite; a program needn't handle non-finite values.
Results may differ from a plain program's by a relative error of at most 0.003.
Values may be sent and summed in bfloat16 or wider, within the bound.
No kernel may reach another device: no remote copies, remote signals or barrier semaphores. Data moves between devices by JAX's collectives and lax.ppermute only.
A program may use at most 64 MiB of HBM per device.

v0:
```python
import jax
import jax.numpy as jnp
from jax import lax
from jax.sharding import PartitionSpec as P

NZ = 16
STEPS = 4


courant = 0.3
slope = 0.6


def passed_along(block, axis, distance):
    devices = range(lax.axis_size(axis))
    route = [((i - distance) % len(devices), i) for i in devices]
    return lax.ppermute(block, axis, route)


def from_partner(block, axis, distance):
    count = lax.axis_size(axis)
    route = []
    for low in range(count):
        high = low | 1 << distance
        if high != low and high < count:
            route += [(low, high), (high, low)]
    return lax.ppermute(block, axis, route)


def shape_step(current, factor):
    return (factor * current.astype(jnp.float32)).astype(jnp.bfloat16)


def one_drift(center, before_cells, after_cells, velocity, component):
    upwind_pos = jnp.maximum(velocity[:, component], 0.0)[:, :, None, None]
    upwind_neg = jnp.minimum(velocity[:, component], 0.0)[:, :, None, None]
    return upwind_pos * (center - before_cells) + upwind_neg * (after_cells - center)


def finish_step(shaped, row_before, row_after, factor, velocity, analysis, synthesis, decay_rates):
    from_left = passed_along(shaped[:, :, -1:], "space", 2)
    from_right = passed_along(shaped[:, :, :1], "space", -2)
    center = shaped.astype(jnp.float32)
    x_before = jnp.concatenate([from_left, shaped[:, :, :-1]], axis=2).astype(jnp.float32)
    x_after = jnp.concatenate([shaped[:, :, 1:], from_right], axis=2).astype(jnp.float32)
    y_before = jnp.concatenate([row_before, shaped[..., :-NZ]], axis=3).astype(jnp.float32)
    y_after = jnp.concatenate([shaped[..., NZ:], row_after], axis=3).astype(jnp.float32)
    z_index = lax.broadcasted_iota(jnp.int32, (1, 1, 1, shaped.shape[3]), 3) % NZ
    z_before = jnp.where(
        z_index == 0, jnp.roll(center, 1 - NZ, axis=3), jnp.roll(center, 1, axis=3)
    )
    z_after = jnp.where(
        z_index == NZ - 1, jnp.roll(center, NZ - 1, axis=3), jnp.roll(center, -1, axis=3)
    )
    drift_sum = one_drift(center, x_before, x_after, velocity, 0)
    drift_sum = drift_sum + one_drift(center, y_before, y_after, velocity, 1)
    drift_sum = drift_sum + one_drift(center, z_before, z_after, velocity, 2)
    moved_cells = (center - courant * drift_sum).astype(jnp.bfloat16)
    harmonics = jnp.einsum(
        "ho,poxm->phxm", analysis, moved_cells, preferred_element_type=jnp.float32
    )
    harmonics = (decay_rates[None, :, None, None] * harmonics).astype(jnp.bfloat16)
    rotated = jnp.mean(moved_cells.astype(jnp.float32), axis=1, keepdims=True) + jnp.einsum(
        "oh,phxm->poxm", synthesis, harmonics, preferred_element_type=jnp.float32
    )
    return (factor * rotated).astype(jnp.bfloat16)


def pair_term(own_slice, partner_slice, weight):
    return weight * jnp.mean(
        own_slice.astype(jnp.float32) * partner_slice.astype(jnp.float32), axis=1
    )


def partition_of(local_total, cell_count):
    return lax.psum(local_total, "space") / cell_count


def shards(fields, end_weights, directions, analysis, synthesis, decay_rates):
    space_index = lax.axis_index("space")
    team_bit = space_index % 2
    is_first = team_bit == 0
    plane_count = fields.shape[0]
    planes = space_index // 2 * plane_count + lax.broadcasted_iota(jnp.int32, (plane_count, 1), 0)
    ramp = slope * planes.astype(jnp.float32) / (plane_count * lax.axis_size("space") // 2)
    partner_field = from_partner(fields, "space", 0)
    own_field = fields + ramp
    other_field = partner_field + ramp
    half_steps = STEPS // 2
    device_cells = fields.shape[0] * fields.shape[1]

    def weight_of(position):
        return 0.5 if position in (0, half_steps) else 1.0

    half_cells = fields.shape[1] // 2
    own_start = team_bit * half_cells
    other_start = (1 - team_bit) * half_cells
    field_a = jnp.where(is_first, own_field, other_field)
    field_b = jnp.where(is_first, other_field, own_field)
    half_field_a = lax.dynamic_slice_in_dim(field_a, own_start, half_cells, 1)
    half_field_b = lax.dynamic_slice_in_dim(field_b, own_start, half_cells, 1)
    own_end = lax.dynamic_slice_in_dim(end_weights, own_start, half_cells, 2)
    partner_end = from_partner(
        lax.dynamic_slice_in_dim(end_weights, other_start, half_cells, 2), "space", 0
    )
    start_a = jnp.where(is_first, own_end, partner_end)
    start_b = jnp.where(is_first, partner_end, own_end)
    current = jnp.stack([start_a, start_b])
    first_factor = jnp.exp(-0.5 * jnp.stack([half_field_a, half_field_b]))[:, None]
    second_factor = jnp.exp(-0.5 * jnp.stack([half_field_b, half_field_a]))[:, None]
    velocity = jnp.stack([directions, -directions])
    slices = [current]
    for step_index in range(STEPS):
        factor = first_factor if step_index < half_steps else second_factor
        shaped = shape_step(current, factor)
        first_row, last_row = from_partner((shaped[..., :NZ], shaped[..., -NZ:]), "space", 0)
        current = finish_step(
            shaped, last_row, first_row, factor, velocity, analysis, synthesis, decay_rates
        )
        slices.append(current)
    density_a = jnp.zeros((1,) + half_field_a.shape, jnp.float32)
    density_b = jnp.zeros((1,) + half_field_a.shape, jnp.float32)
    for position in range(half_steps + 1):
        density_a = density_a + pair_term(
            slices[position][0:1], slices[STEPS - position][1:2], weight_of(position)
        )
        density_b = density_b + pair_term(
            slices[position][1:2], slices[STEPS - position][0:1], weight_of(position)
        )
    local_total = jnp.sum(pair_term(slices[half_steps][0:1], slices[half_steps][1:2], 1.0))
    partition = partition_of(local_total, lax.axis_size("space") * device_cells // 2)
    kept_half = jnp.where(is_first, density_a, density_b)[0] / partition
    sent_half = jnp.where(is_first, density_b, density_a)[0] / partition
    received = from_partner(sent_half, "space", 0)
    density = jnp.where(
        is_first,
        jnp.concatenate([kept_half, received], axis=1),
        jnp.concatenate([received, kept_half], axis=1),
    )
    return density


def solution(mesh):
    return jax.shard_map(
        shards,
        mesh=mesh,
        in_specs=(P(("runs", "space"), None), P(None, ("runs", "space"), None), P(), P(), P(), P()),
        out_specs=P(("runs", "space"), None),
        check_vma=False,
    )
```

profile of v0, /device:TPU:0, one launch (start us, length us, event | category | flops | bytes accessed | tf_op | source)
XLA Modules:
  0.0 133.5 jit_solution(3149761447200398039)
XLA Ops:
  0.5 1.6 %constant_dynamic-slice_fusion.1 = (bf16[256,4,256]{2,1,0:T(4,128)(2,1)S(1)}, bf16[256,4,256]{2,1,0:T(4,128)(2,1)S(1)}) fusion(bf16[256,4,512]{2,1,0:T(4,128)(2,1)} %param.7, s32[]{:T(128)S(6)} %select_n.128, s32[]{:T(128)S(6)} %select_n.129), kind=kLoop, calls=%fused_computation.167 | loop fusion | bytes 2097160 | tf_op jit(solution)/shard_map/dynamic_slice | solution.py:102
  3.2 1.2 collective-permute-done
  5.8 2.7 %collective-permute-start.2 = (bf16[2,256,1,256]{1,3,2,0:T(8,128)(2,1)S(1)}, bf16[2,256,1,256]{1,3,2,0:T(8,128)(2,1)S(1)}, u32[]{:S(2)}, u32[]{:S(2)}) collective-permute-start(bf16[2,256,1,256]{1,3,2,0:T(8,128)(2,1)S(1)} %get-tuple-element.71), channel_id=1, source_target_pairs={{14,0},{15,1},{0,2},{1,3},{2,4},{3,5},{4,6},{5,7},{6,8},{7,9},{8,1... | collective-permute-start | bytes 786440 | tf_op jit(solution)/shard_map/ppermute | solution.py:17
  8.6 3.1 %collective-permute-start.3 = (bf16[2,256,1,256]{1,3,2,0:T(8,128)(2,1)S(1)}, bf16[2,256,1,256]{1,3,2,0:T(8,128)(2,1)S(1)}, u32[]{:S(2)}, u32[]{:S(2)}) collective-permute-start(bf16[2,256,1,256]{1,3,2,0:T(8,128)(2,1)S(1)} %get-tuple-element.72), channel_id=1, source_target_pairs={{2,0},{3,1},{4,2},{5,3},{6,4},{7,5},{8,6},{9,7},{10,8},{11,9},{12,... | collective-permute-start | bytes 786440 | tf_op jit(solution)/shard_map/ppermute | solution.py:17
  12.3 0.7 collective-permute-done.4
  13.2 7.1 %collective-permute-done.2 = bf16[2,256,1,256]{1,3,2,0:T(8,128)(2,1)S(1)} collective-permute-done((bf16[2,256,1,256]{1,3,2,0:T(8,128)(2,1)S(1)}, bf16[2,256,1,256]{1,3,2,0:T(8,128)(2,1)S(1)}, u32[]{:S(2)}, u32[]{:S(2)}) %collective-permute-start.2) | collective-permute-done | bytes 262176 | tf_op jit(solution)/shard_map/ppermute | solution.py:17
  20.3 2.2 %collective-permute-done.3 = bf16[2,256,1,256]{1,3,2,0:T(8,128)(2,1)S(1)} collective-permute-done((bf16[2,256,1,256]{1,3,2,0:T(8,128)(2,1)S(1)}, bf16[2,256,1,256]{1,3,2,0:T(8,128)(2,1)S(1)}, u32[]{:S(2)}, u32[]{:S(2)}) %collective-permute-start.3) | collective-permute-done | bytes 262176 | tf_op jit(solution)/shard_map/ppermute | solution.py:17
  22.5 5.3 %convert_reduce_fusion.3 = (f32[2,4,256]{2,1,0:T(4,128)S(1)}, bf16[2,256,4,256]{1,3,2,0:T(8,128)(2,1)S(1)}) fusion(f32[2,256,4,1]{1,3,2,0:T(1,128)S(1)} %get-tuple-element.84, f32[2,256,4,255]{1,3,2,0:T(8,128)S(1)} %get-tuple-element.86, f32[2,256,4,241]{1,3,2,0:T(8,128)S(1)} %get-tuple-element.80, f32[2,256,4,15]{1,3,2,0:T(8,128)S(1)} %get-tuple-element.82, ...), kind=kLoop, calls=%fused_computation.98 | loop fusion | flops 26736640 | bytes 14709248 | tf_op jit(solution)/shard_map/reduce_sum | solution.py:63
  27.8 2.2 %multiply_convert_fusion.8 = (bf16[2,256,4,256]{1,3,2,0:T(8,128)(2,1)S(1)}, bf16[2,256,4,256]{1,3,2,0:T(8,128)(2,1)}) fusion(f32[2,4,256]{2,1,0:T(4,128)S(1)} %get-tuple-element.96, bf16[256,256]{1,0:T(8,128)(2,1)S(1)} %copy-done, bf16[2,256,4,256]{1,3,2,0:T(8,128)(2,1)S(1)} %get-tuple-element.16, f32[256]{0:T(256)S(1)} %copy-done.19, ...), kind=kOutput, calls=%fused_computation.95 | convolution fusion | flops 541065216 | bytes 3425280 | tf_op jit(solution)/shard_map/oh,phxm->poxm/dot_general | solution.py:63
  31.4 4.4 %collective-permute-start.7 = (bf16[2,256,1,256]{1,3,2,0:T(8,128)(2,1)S(1)}, bf16[2,256,1,256]{1,3,2,0:T(8,128)(2,1)S(1)}, u32[]{:S(2)}, u32[]{:S(2)}) collective-permute-start(bf16[2,256,1,256]{1,3,2,0:T(8,128)(2,1)S(1)} %get-tuple-element.56), channel_id=1, source_target_pairs={{2,0},{3,1},{4,2},{5,3},{6,4},{7,5},{8,6},{9,7},{10,8},{11,9},{12,... | collective-permute-start | bytes 786440 | tf_op jit(solution)/shard_map/ppermute | solution.py:17
  36.4 0.7 collective-permute-done.8
  37.3 5.0 %collective-permute-done.6 = bf16[2,256,1,256]{1,3,2,0:T(8,128)(2,1)S(1)} collective-permute-done((bf16[2,256,1,256]{1,3,2,0:T(8,128)(2,1)S(1)}, bf16[2,256,1,256]{1,3,2,0:T(8,128)(2,1)S(1)}, u32[]{:S(2)}, u32[]{:S(2)}) %collective-permute-start.6) | collective-permute-done | bytes 262176 | tf_op jit(solution)/shard_map/ppermute | solution.py:17
  42.3 3.3 %collective-permute-done.7 = bf16[2,256,1,256]{1,3,2,0:T(8,128)(2,1)S(1)} collective-permute-done((bf16[2,256,1,256]{1,3,2,0:T(8,128)(2,1)S(1)}, bf16[2,256,1,256]{1,3,2,0:T(8,128)(2,1)S(1)}, u32[]{:S(2)}, u32[]{:S(2)}) %collective-permute-start.7) | collective-permute-done | bytes 262176 | tf_op jit(solution)/shard_map/ppermute | solution.py:17
  45.7 4.9 %convert_reduce_fusion.2 = (f32[2,4,256]{2,1,0:T(4,128)S(1)}, bf16[2,256,4,256]{1,3,2,0:T(8,128)(2,1)S(1)}) fusion(f32[2,256,4,1]{1,3,2,0:T(1,128)S(1)} %get-tuple-element.68, f32[2,256,4,255]{1,3,2,0:T(8,128)S(1)} %get-tuple-element.70, f32[2,256,4,241]{1,3,2,0:T(8,128)S(1)} %get-tuple-element.64, f32[2,256,4,15]{1,3,2,0:T(8,128)S(1)} %get-tuple-element.66, ...), kind=kLoop, calls=%fused_computation.94 | loop fusion | flops 23590912 | bytes 14701056 | tf_op jit(solution)/shard_map/reduce_sum | solution.py:63
  50.6 2.2 %multiply_convert_fusion.5 = (bf16[2,256,4,256]{1,3,2,0:T(8,128)(2,1)S(1)}, bf16[2,256,4,256]{1,3,2,0:T(8,128)(2,1)}) fusion(f32[2,4,256]{2,1,0:T(4,128)S(1)} %get-tuple-element.95, bf16[256,256]{1,0:T(8,128)(2,1)S(1)} %copy-done, bf16[2,256,4,256]{1,3,2,0:T(8,128)(2,1)S(1)} %get-tuple-element.14, f32[256]{0:T(256)S(1)} %copy-done.19, ...), kind=kOutput, calls=%fused_computation.91 | convolution fusion | flops 541065216 | bytes 3433472 | tf_op jit(solution)/shard_map/oh,phxm->poxm/dot_general | solution.py:63
  52.8 0.7 fusion.92
  53.5 0.8 fusion.90
  54.4 1.4 %fusion.91 = (bf16[2,256,3,256]{1,3,2,0:T(8,128)(2,1)}, bf16[2,256,3,256]{1,3,2,0:T(8,128)(2,1)}) fusion(bf16[2,256,4,256]{1,3,2,0:T(8,128)(2,1)S(1)} %get-tuple-element.105), kind=kLoop, calls=%fused_computation.180 | loop fusion | bytes 3145728 | tf_op jit(solution)/shard_map/slice | solution.py:44
  55.8 1.1 fusion.93
  56.8 2.3 %fusion.94 = (f32[2,256,4,241]{1,3,2,0:T(8,128)}, f32[2,256,4,241]{1,3,2,0:T(8,128)}) fusion(bf16[2,256,4,256]{1,3,2,0:T(8,128)(2,1)S(1)} %get-tuple-element.105), kind=kLoop, calls=%fused_computation.183 | loop fusion | bytes 7897088 | tf_op jit(solution)/shard_map/jit(_roll_static)/slice | solution.py:50
  59.2 2.4 %fusion.97 = (f32[2,256,4,255]{1,3,2,0:T(8,128)}, f32[2,256,4,255]{1,3,2,0:T(8,128)}) fusion(bf16[2,256,4,256]{1,3,2,0:T(8,128)(2,1)S(1)} %get-tuple-element.105), kind=kLoop, calls=%fused_computation.186 | loop fusion | bytes 8355840 | tf_op jit(solution)/shard_map/jit(_roll_static)/slice | solution.py:50
  61.8 4.7 %collective-permute-start.11 = (bf16[2,256,1,256]{1,3,2,0:T(8,128)(2,1)}, bf16[2,256,1,256]{1,3,2,0:T(8,128)(2,1)}, u32[]{:S(2)}, u32[]{:S(2)}) collective-permute-start(bf16[2,256,1,256]{1,3,2,0:T(8,128)(2,1)} %get-tuple-element.40), channel_id=1, source_target_pairs={{2,0},{3,1},{4,2},{5,3},{6,4},{7,5},{8,6},{9,7},{10,8},{11,9},{12,... | collective-permute-start | bytes 786440 | tf_op jit(solution)/shard_map/ppermute | solution.py:17
  67.6 0.6 fusion.96
  68.2 31.1 %psum.7 = f32[]{:T(128)} all-reduce(f32[]{:T(128)} %multiply_reduce_fusion.5), channel_id=1, replica_groups=mesh['runs'=2,'space'=16] {'space'}, use_global_device_ids=true, to_apply=%region_10.11 | all-reduce | flops 1 | bytes 8 | tf_op jit(solution)/shard_map/psum | solution.py:76
  99.9 8.4 %convert_reduce_fusion.1 = (f32[2,4,256]{2,1,0:T(4,128)S(1)}, bf16[2,256,4,256]{1,3,2,0:T(8,128)(2,1)}) fusion(f32[2,256,4,1]{1,3,2,0:T(1,128)} %get-tuple-element.52, f32[2,256,4,255]{1,3,2,0:T(8,128)} %get-tuple-element.54, f32[2,256,4,241]{1,3,2,0:T(8,128)} %get-tuple-element.48, f32[2,256,4,15]{1,3,2,0:T(8,128)S(1)} %get-tuple-element.50, ...), kind=kLoop, calls=%fused_computation.90 | loop fusion | flops 23590912 | bytes 14701056 | tf_op jit(solution)/shard_map/reduce_sum | solution.py:63
  108.3 2.6 %multiply_convert_fusion.2 = (bf16[2,256,4,256]{1,3,2,0:T(8,128)(2,1)S(1)}, bf16[2,256,4,256]{1,3,2,0:T(8,128)(2,1)S(1)}) fusion(f32[2,4,256]{2,1,0:T(4,128)} %copy-done.14, bf16[256,256]{1,0:T(8,128)(2,1)S(1)} %copy-done, bf16[2,256,4,256]{1,3,2,0:T(8,128)(2,1)} %get-tuple-element.12, f32[256]{0:T(256)} %param.11, bf16[256,256]{1,0:T(8,128)(2,1)} %param.9, ...), kind=kOutput, calls=%fused_computation.87 | convolution fusion | flops 541065216 | bytes 3425280 | tf_op jit(solution)/shard_map/oh,phxm->poxm/dot_general | solution.py:63
  112.1 4.7 %collective-permute-start.15 = (bf16[2,256,1,256]{1,3,2,0:T(8,128)(2,1)S(1)}, bf16[2,256,1,256]{1,3,2,0:T(8,128)(2,1)S(1)}, u32[]{:S(2)}, u32[]{:S(2)}) collective-permute-start(bf16[2,256,1,256]{1,3,2,0:T(8,128)(2,1)S(1)} %get-tuple-element.24), channel_id=1, source_target_pairs={{2,0},{3,1},{4,2},{5,3},{6,4},{7,5},{8,6},{9,7},{10,8},{11,9},{12,... | collective-permute-start | bytes 786440 | tf_op jit(solution)/shard_map/ppermute | solution.py:17
  118.3 3.8 %collective-permute-done.14 = bf16[2,256,1,256]{1,3,2,0:T(8,128)(2,1)S(1)} collective-permute-done((bf16[2,256,1,256]{1,3,2,0:T(8,128)(2,1)S(1)}, bf16[2,256,1,256]{1,3,2,0:T(8,128)(2,1)S(1)}, u32[]{:S(2)}, u32[]{:S(2)}) %collective-permute-start.14) | collective-permute-done | bytes 262176 | tf_op jit(solution)/shard_map/ppermute | solution.py:17
  122.1 3.1 %collective-permute-done.15 = bf16[2,256,1,256]{1,3,2,0:T(8,128)(2,1)S(1)} collective-permute-done((bf16[2,256,1,256]{1,3,2,0:T(8,128)(2,1)S(1)}, bf16[2,256,1,256]{1,3,2,0:T(8,128)(2,1)S(1)}, u32[]{:S(2)}, u32[]{:S(2)}) %collective-permute-start.15) | collective-permute-done | bytes 262176 | tf_op jit(solution)/shard_map/ppermute | solution.py:17
  125.3 4.9 %convert_reduce_fusion = (f32[2,4,256]{2,1,0:T(4,128)S(1)}, bf16[2,256,4,256]{1,3,2,0:T(8,128)(2,1)S(1)}) fusion(f32[2,256,4,1]{1,3,2,0:T(1,128)S(1)} %get-tuple-element.36, f32[2,256,4,255]{1,3,2,0:T(8,128)S(1)} %get-tuple-element.38, f32[2,256,4,241]{1,3,2,0:T(8,128)S(1)} %get-tuple-element.32, f32[2,256,4,15]{1,3,2,0:T(8,128)S(1)} %get-tuple-element.34, ...), kind=kLoop, calls=%fused_computation.86 | loop fusion | flops 23590912 | bytes 14701056 | tf_op jit(solution)/shard_map/reduce_sum | solution.py:63
  130.3 1.0 fusion.59
  131.7 1.2 collective-permute-done.18
  (117 shorter events, 10.9 us)
Async XLA Ops:
  0.0 27.7 %copy-start = (bf16[256,256]{1,0:T(8,128)(2,1)S(1)}, bf16[256,256]{1,0:T(8,128)(2,1)}, u32[]{:S(2)}) copy-start(bf16[256,256]{1,0:T(8,128)(2,1)} %param.10) | copy-start | bytes 393220
  0.0 3.0 %collective-permute-start.1 = (f32[4,512]{1,0:T(4,128)}, f32[4,512]{1,0:T(4,128)S(1)}, u32[]{:S(2)}, u32[]{:S(2)}) collective-permute-start(f32[4,512]{1,0:T(4,128)} %param.6), channel_id=1, source_target_pairs={{0,1},{1,0},{2,3},{3,2},{4,5},{5,4},{6,7},{7,6},{8,9},{9,8},{10,11... | collective-permute-start | bytes 24584 | tf_op jit(solution)/shard_map/ppermute | solution.py:27
  2.4 2.0 %collective-permute-start = (bf16[256,4,256]{0,2,1:T(8,128)(2,1)S(1)}, bf16[256,4,256]{0,2,1:T(8,128)(2,1)S(1)}, u32[]{:S(2)}, u32[]{:S(2)}) collective-permute-start(bf16[256,4,256]{0,2,1:T(8,128)(2,1)S(1)} %copy.26), channel_id=1, source_target_pairs={{0,1},{1,0},{2,3},{3,2},{4,5},{5,4},{6,7},{7,6},{8,9},{9,8},{10,11... | collective-permute-start | bytes 1572872 | tf_op jit(solution)/shard_map/ppermute | solution.py:27
  2.5 43.1 %copy-start.10 = (pred[256]{0:T(512)(128)(4,1)}, pred[256]{0:T(512)(128)(4,1)S(1)}, u32[]{:S(2)}) copy-start(pred[256]{0:T(512)(128)(4,1)S(1)} %get-tuple-element.109) | copy-start | bytes 772
  2.5 43.1 %copy-start.12 = (pred[256]{0:T(512)(128)(4,1)}, pred[256]{0:T(512)(128)(4,1)S(1)}, u32[]{:S(2)}) copy-start(pred[256]{0:T(512)(128)(4,1)S(1)} %get-tuple-element.110) | copy-start | bytes 772
  2.6 43.0 %copy-start.3 = (f32[2,256]{1,0:T(2,128)}, f32[2,256]{1,0:T(2,128)S(1)}, u32[]{:S(2)}) copy-start(f32[2,256]{1,0:T(2,128)S(1)} %get-tuple-element.111) | copy-start | bytes 6148
  2.6 43.0 %copy-start.5 = (f32[2,256]{1,0:T(2,128)}, f32[2,256]{1,0:T(2,128)S(1)}, u32[]{:S(2)}) copy-start(f32[2,256]{1,0:T(2,128)S(1)} %get-tuple-element.112) | copy-start | bytes 6148
  3.1 47.5 %copy-start.14 = (f32[2,4,256]{2,1,0:T(4,128)}, f32[2,4,256]{2,1,0:T(4,128)S(1)}, u32[]{:S(2)}) copy-start(f32[2,4,256]{2,1,0:T(4,128)S(1)} %get-tuple-element.95) | copy-start | bytes 24580
  5.8 14.4 %collective-permute-start.2 = (bf16[2,256,1,256]{1,3,2,0:T(8,128)(2,1)S(1)}, bf16[2,256,1,256]{1,3,2,0:T(8,128)(2,1)S(1)}, u32[]{:S(2)}, u32[]{:S(2)}) collective-permute-start(bf16[2,256,1,256]{1,3,2,0:T(8,128)(2,1)S(1)} %get-tuple-element.71), channel_id=1, source_target_pairs={{14,0},{15,1},{0,2},{1,3},{2,4},{3,5},{4,6},{5,7},{6,8},{7,9},{8,1... | collective-permute-start | bytes 786440 | tf_op jit(solution)/shard_map/ppermute | solution.py:17
  8.6 13.9 %collective-permute-start.3 = (bf16[2,256,1,256]{1,3,2,0:T(8,128)(2,1)S(1)}, bf16[2,256,1,256]{1,3,2,0:T(8,128)(2,1)S(1)}, u32[]{:S(2)}, u32[]{:S(2)}) collective-permute-start(bf16[2,256,1,256]{1,3,2,0:T(8,128)(2,1)S(1)} %get-tuple-element.72), channel_id=1, source_target_pairs={{2,0},{3,1},{4,2},{5,3},{6,4},{7,5},{8,6},{9,7},{10,8},{11,9},{12,... | collective-permute-start | bytes 786440 | tf_op jit(solution)/shard_map/ppermute | solution.py:17
  11.7 1.3 collective-permute-start.4
  11.8 1.3 collective-permute-start.5
  22.5 5.3 %copy-start.19 = (f32[256]{0:T(256)S(1)}, f32[256]{0:T(256)}, u32[]{:S(2)}) copy-start(f32[256]{0:T(256)} %param.11) | copy-start | bytes 3076
  31.1 11.3 %collective-permute-start.6 = (bf16[2,256,1,256]{1,3,2,0:T(8,128)(2,1)S(1)}, bf16[2,256,1,256]{1,3,2,0:T(8,128)(2,1)S(1)}, u32[]{:S(2)}, u32[]{:S(2)}) collective-permute-start(bf16[2,256,1,256]{1,3,2,0:T(8,128)(2,1)S(1)} %get-tuple-element.55), channel_id=1, source_target_pairs={{14,0},{15,1},{0,2},{1,3},{2,4},{3,5},{4,6},{5,7},{6,8},{7,9},{8,1... | collective-permute-start | bytes 786440 | tf_op jit(solution)/shard_map/ppermute | solution.py:17
  31.4 14.2 %collective-permute-start.7 = (bf16[2,256,1,256]{1,3,2,0:T(8,128)(2,1)S(1)}, bf16[2,256,1,256]{1,3,2,0:T(8,128)(2,1)S(1)}, u32[]{:S(2)}, u32[]{:S(2)}) collective-permute-start(bf16[2,256,1,256]{1,3,2,0:T(8,128)(2,1)S(1)} %get-tuple-element.56), channel_id=1, source_target_pairs={{2,0},{3,1},{4,2},{5,3},{6,4},{7,5},{8,6},{9,7},{10,8},{11,9},{12,... | collective-permute-start | bytes 786440 | tf_op jit(solution)/shard_map/ppermute | solution.py:17
  35.9 1.3 collective-permute-start.8
  35.9 1.4 %collective-permute-start.9 = (bf16[2,256,4,16]{1,3,2,0:T(8,128)(2,1)S(1)}, bf16[2,256,4,16]{1,3,2,0:T(8,128)(2,1)S(1)}, u32[]{:S(2)}, u32[]{:S(2)}) collective-permute-start(bf16[2,256,4,16]{1,3,2,0:T(8,128)(2,1)S(1)} %get-tuple-element.60), channel_id=1, source_target_pairs={{0,1},{1,0},{2,3},{3,2},{4,5},{5,4},{6,7},{7,6},{8,9},{9,8},{10,11... | collective-permute-start | bytes 196616 | tf_op jit(solution)/shard_map/ppermute | solution.py:27
  61.7 5.4 %copy-start.7 = (f32[4,256]{1,0:T(4,128)}, f32[4,256]{1,0:T(4,128)S(1)}, u32[]{:S(2)}) copy-start(f32[4,256]{1,0:T(4,128)S(1)} %multiply_reduce_fusion.2) | copy-start | bytes 12292
  61.7 38.2 %collective-permute-start.10 = (bf16[2,256,1,256]{1,3,2,0:T(8,128)(2,1)}, bf16[2,256,1,256]{1,3,2,0:T(8,128)(2,1)}, u32[]{:S(2)}, u32[]{:S(2)}) collective-permute-start(bf16[2,256,1,256]{1,3,2,0:T(8,128)(2,1)} %get-tuple-element.39), channel_id=1, source_target_pairs={{14,0},{15,1},{0,2},{1,3},{2,4},{3,5},{4,6},{5,7},{6,8},{7,9},{8,1... | collective-permute-start | bytes 786440 | tf_op jit(solution)/shard_map/ppermute | solution.py:17
  61.8 38.1 %collective-permute-start.11 = (bf16[2,256,1,256]{1,3,2,0:T(8,128)(2,1)}, bf16[2,256,1,256]{1,3,2,0:T(8,128)(2,1)}, u32[]{:S(2)}, u32[]{:S(2)}) collective-permute-start(bf16[2,256,1,256]{1,3,2,0:T(8,128)(2,1)} %get-tuple-element.40), channel_id=1, source_target_pairs={{2,0},{3,1},{4,2},{5,3},{6,4},{7,5},{8,6},{9,7},{10,8},{11,9},{12,... | collective-permute-start | bytes 786440 | tf_op jit(solution)/shard_map/ppermute | solution.py:17
  67.1 32.8 %collective-permute-start.12 = (bf16[2,256,4,16]{1,3,2,0:T(8,128)(2,1)}, bf16[2,256,4,16]{1,3,2,0:T(8,128)(2,1)S(1)}, u32[]{:S(2)}, u32[]{:S(2)}) collective-permute-start(bf16[2,256,4,16]{1,3,2,0:T(8,128)(2,1)} %get-tuple-element.43), channel_id=1, source_target_pairs={{0,1},{1,0},{2,3},{3,2},{4,5},{5,4},{6,7},{7,6},{8,9},{9,8},{10,11... | collective-permute-start | bytes 196616 | tf_op jit(solution)/shard_map/ppermute | solution.py:27
  67.1 32.8 %collective-permute-start.13 = (bf16[2,256,4,16]{1,3,2,0:T(8,128)(2,1)}, bf16[2,256,4,16]{1,3,2,0:T(8,128)(2,1)}, u32[]{:S(2)}, u32[]{:S(2)}) collective-permute-start(bf16[2,256,4,16]{1,3,2,0:T(8,128)(2,1)} %get-tuple-element.44), channel_id=1, source_target_pairs={{0,1},{1,0},{2,3},{3,2},{4,5},{5,4},{6,7},{7,6},{8,9},{9,8},{10,11... | collective-permute-start | bytes 196616 | tf_op jit(solution)/shard_map/ppermute | solution.py:27
  111.6 5.8 %copy-start.1 = (bf16[2,256,4,256]{1,3,2,0:T(8,128)(2,1)S(1)}, bf16[2,256,4,256]{1,3,2,0:T(8,128)(2,1)}, u32[]{:S(2)}) copy-start(bf16[2,256,4,256]{1,3,2,0:T(8,128)(2,1)} %get-tuple-element.104) | copy-start | bytes 3145732
  112.0 13.2 %copy-start.4 = (f32[2,256]{1,0:T(2,128)S(1)}, f32[2,256]{1,0:T(2,128)}, u32[]{:S(2)}) copy-start(f32[2,256]{1,0:T(2,128)} %copy-done.3) | copy-start | bytes 6148
  112.0 13.2 %copy-start.6 = (f32[2,256]{1,0:T(2,128)S(1)}, f32[2,256]{1,0:T(2,128)}, u32[]{:S(2)}) copy-start(f32[2,256]{1,0:T(2,128)} %copy-done.5) | copy-start | bytes 6148
  112.0 13.2 %copy-start.11 = (pred[256]{0:T(512)(128)(4,1)S(1)}, pred[256]{0:T(512)(128)(4,1)}, u32[]{:S(2)}) copy-start(pred[256]{0:T(512)(128)(4,1)} %copy-done.10) | copy-start | bytes 772
  112.0 13.2 %copy-start.13 = (pred[256]{0:T(512)(128)(4,1)S(1)}, pred[256]{0:T(512)(128)(4,1)}, u32[]{:S(2)}) copy-start(pred[256]{0:T(512)(128)(4,1)} %copy-done.12) | copy-start | bytes 772
  112.1 10.1 %collective-permute-start.14 = (bf16[2,256,1,256]{1,3,2,0:T(8,128)(2,1)S(1)}, bf16[2,256,1,256]{1,3,2,0:T(8,128)(2,1)S(1)}, u32[]{:S(2)}, u32[]{:S(2)}) collective-permute-start(bf16[2,256,1,256]{1,3,2,0:T(8,128)(2,1)S(1)} %get-tuple-element.23), channel_id=1, source_target_pairs={{14,0},{15,1},{0,2},{1,3},{2,4},{3,5},{4,6},{5,7},{6,8},{7,9},{8,1... | collective-permute-start | bytes 786440 | tf_op jit(solution)/shard_map/ppermute | solution.py:17
  112.1 13.1 %collective-permute-start.15 = (bf16[2,256,1,256]{1,3,2,0:T(8,128)(2,1)S(1)}, bf16[2,256,1,256]{1,3,2,0:T(8,128)(2,1)S(1)}, u32[]{:S(2)}, u32[]{:S(2)}) collective-permute-start(bf16[2,256,1,256]{1,3,2,0:T(8,128)(2,1)S(1)} %get-tuple-element.24), channel_id=1, source_target_pairs={{2,0},{3,1},{4,2},{5,3},{6,4},{7,5},{8,6},{9,7},{10,8},{11,9},{12,... | collective-permute-start | bytes 786440 | tf_op jit(solution)/shard_map/ppermute | solution.py:17
  116.8 1.3 collective-permute-start.16
  116.9 1.4 %collective-permute-start.17 = (bf16[2,256,4,16]{1,3,2,0:T(8,128)(2,1)S(1)}, bf16[2,256,4,16]{1,3,2,0:T(8,128)(2,1)S(1)}, u32[]{:S(2)}, u32[]{:S(2)}) collective-permute-start(bf16[2,256,4,16]{1,3,2,0:T(8,128)(2,1)S(1)} %get-tuple-element.28), channel_id=1, source_target_pairs={{0,1},{1,0},{2,3},{3,2},{4,5},{5,4},{6,7},{7,6},{8,9},{9,8},{10,11... | collective-permute-start | bytes 196616 | tf_op jit(solution)/shard_map/ppermute | solution.py:27
  131.7 1.2 collective-permute-start.18
  (8 other events, 29.1 us)
where the time goes:
time: 134 us; the launch traced here: 133 us
  blocking collectives  31.1 us (23%)
  waiting for transfers between devices  29.2 us (22%)
  other arithmetic  26.2 us (20%)
  starting transfers between devices  23 us (17%)
  local copies, waits for them, and re-layouts  14.7 us (11%)
  matrix products  8.01 us (6%)
    psum x1, blocking collectives, partition_of(): return lax.psum(local_total, 'space') / cell_count  31.1 us
    ppermute x8, waiting for transfers between devices, passed_along(): return lax.ppermute(block, axis, route)  24.5 us
    reduce_sum x4, other arithmetic, finish_step(): jnp.mean(moved_cells.astype(jnp.float32), axis=1, keepdims=True)  23.5 us
    ppermute x8, starting transfers between devices, passed_along(): return lax.ppermute(block, axis, route)  20.1 us
    dot_general x4, matrix products, finish_step(): jnp.einsum('oh,phxm->poxm', synthesis, harmonics, preferred_element_type=...  8.01 us
    ppermute x11, waiting for transfers between devices, from_partner(): return lax.ppermute(block, axis, route)  4.66 us
    slice x8, local copies, waits for them, and re-layouts, finish_step(): jnp.roll(center, 1, axis=3)  4.09 us
    slice x8, local copies, waits for them, and re-layouts, finish_step(): jnp.roll(center, 1 - NZ, axis=3)  3.42 us
  transfers between devices with their start and end apart: 19, of which 14 were waited for; matrix products, arithmetic and copies ran while one was open for 3% of the time, Pallas kernels for 0%

commit v1 on v0

v1 whole, which is shorter than its diff:
```python
import functools

import jax
import jax.numpy as jnp
from jax import lax
from jax.experimental import pallas as pl
from jax.experimental.pallas import tpu as pltpu
from jax.sharding import PartitionSpec as P

NZ = 16
STEPS = 4
LANES = 128
ROWS = 64

courant = 0.3
slope = 0.6

BF16 = jnp.bfloat16
F32 = jnp.float32


def swap_species(block):
    count = lax.axis_size("space")
    return lax.ppermute(block, "space", [(i ^ 1, i) for i in range(count)])


def to_next_slab(block):
    count = lax.axis_size("space")
    return lax.ppermute(block, "space", [(i, (i + (2 if i % 2 == 0 else -2)) % count) for i in range(count)])


def rows_of(index):
    return pl.ds(pl.multiple_of(index * ROWS, ROWS), ROWS)


def columns(tile):
    return slice(LANES * tile, LANES * (tile + 1))


def geometry(v_ref, rows):
    lane = lax.broadcasted_iota(jnp.int32, (ROWS, LANES), 1)
    vx, vy, vz = (v_ref[c, rows, :] for c in range(3))
    plus_x, plus_y, plus_z = vx > 0, vy > 0, vz > 0
    rate_x, rate_y, rate_z = (courant * jnp.abs(t) for t in (vx, vy, vz))
    stay = 1.0 - (rate_x + rate_y + rate_z)
    z_from = (lane & (LANES - NZ)) | (jnp.where(plus_z, lane - 1, lane + 1) & (NZ - 1))
    y_from = jnp.where(plus_y, lane - NZ, lane + NZ) & (LANES - 1)
    y_edge = jnp.where(plus_y, lane, LANES - 1 - lane) < NZ
    return plus_x, plus_y, stay, rate_x, rate_y, rate_z, z_from, y_from, y_edge


def pick(tile, index):
    return jnp.take_along_axis(tile, index, axis=1)


def load_plane(ref, plane, rows):
    return [ref[plane, rows, columns(t)].astype(F32) for t in range(ref.shape[2] // LANES)]


def drift(center, before, after, geo):
    plus_x, plus_y, stay, rate_x, rate_y, rate_z, z_from, y_from, y_edge = geo
    tiles = len(center)
    turned = [pick(tile, y_from) for tile in center]
    moved = []
    for t in range(tiles):
        total = stay * center[t]
        if before is not None and after is not None:
            total = total + rate_x * jnp.where(plus_x, before[t], after[t])
        elif before is not None:
            total = total + jnp.where(plus_x, rate_x, 0.0) * before[t]
        elif after is not None:
            total = total + jnp.where(plus_x, 0.0, rate_x) * after[t]
        over = jnp.where(plus_y, turned[t - 1], turned[(t + 1) % tiles])
        total = total + rate_y * jnp.where(y_edge, over, turned[t])
        total = total + rate_z * pick(center[t], z_from)
        moved.append(total)
    return moved


def store_plane(ref, plane, rows, tiles):
    for t, tile in enumerate(tiles):
        ref[plane, rows, columns(t)] = tile.astype(ref.dtype)


def mix(matrix, moved):
    return jnp.dot(matrix, moved, preferred_element_type=F32)


def boltzmann(field):
    return jnp.exp(-0.5 * field)


def alone_kernel(start_ref, first_ref, second_ref, v_ref, m_ref, out_ref, edges_ref, held, moved):
    planes, orient, _ = start_ref.shape
    first = boltzmann(first_ref[...])
    second = boltzmann(second_ref[...])

    def write_edge(step, loaded, rows, plus_x):
        for t in range(len(loaded[0])):
            edges_ref[step, rows, columns(t)] = jnp.where(plus_x, loaded[-1][t], loaded[0][t]).astype(BF16)

    for p in range(planes):
        held[p] = (first[p : p + 1] * start_ref[p].astype(F32)).astype(BF16)

    def advance(step, targets, factor):
        @pl.loop(0, orient // ROWS)
        def _(index):
            rows = rows_of(index)
            geo = geometry(v_ref, rows)
            loaded = [load_plane(held, p, rows) for p in range(planes)]
            if step > 0:
                write_edge(step - 1, loaded, rows, geo[0])
            for p in targets:
                before = loaded[p - 1] if p > 0 else None
                after = loaded[p + 1] if p < planes - 1 else None
                store_plane(moved, p, rows, drift(loaded[p], before, after, geo))

        for p in targets:
            held[p] = (factor[p : p + 1] * mix(m_ref[...], moved[p])).astype(BF16)

    advance(0, range(planes), first * first)
    out_ref[...] = held[...]
    advance(1, range(planes), first * second)
    advance(2, (0, planes - 1), second * second)

    @pl.loop(0, orient // ROWS)
    def _(index):
        rows = rows_of(index)
        faces = [load_plane(held, p, rows) for p in (0, planes - 1)]
        write_edge(2, faces, rows, v_ref[0, rows, :] > 0)


def face_parts(v_ref, rows):
    vx = v_ref[0, rows, :]
    rate = courant * jnp.abs(vx)
    return v_ref[3, rows, :] > 0, jnp.where(vx > 0, rate, 0.0), jnp.where(vx > 0, 0.0, rate)


def face_drifts(v_ref, mine_ref, other_ref, moved, slots):
    @pl.loop(0, v_ref.shape[1] // ROWS)
    def _(index):
        rows = rows_of(index)
        ahead, rate_plus, rate_minus = face_parts(v_ref, rows)
        for t in range(mine_ref.shape[1] // LANES):
            mine = mine_ref[rows, columns(t)].astype(F32)
            other = other_ref[rows, columns(t)].astype(F32)
            face = jnp.where(ahead, mine, other)
            moved[slots[0], rows, columns(t)] = (rate_plus * face).astype(BF16)
            moved[slots[1], rows, columns(t)] = (rate_minus * face).astype(BF16)


def second_step_kernel(
    alone_ref, edge_ref, mine_ref, other_ref, first_ref, second_ref, beyond_ref, v_ref, m_ref, out_ref, next_ref, held, moved
):
    planes, orient, _ = alone_ref.shape
    matrix = m_ref[...]
    first, second = boltzmann(first_ref[...]), boltzmann(second_ref[...])
    beyond = boltzmann(beyond_ref[...])
    face_drifts(v_ref, mine_ref, other_ref, moved, (0, 1))

    @pl.loop(0, orient // ROWS)
    def _(index):
        rows = rows_of(index)
        _, rate_plus, rate_minus = face_parts(v_ref, rows)
        for t in range(edge_ref.shape[1] // LANES):
            edge = edge_ref[rows, columns(t)].astype(F32)
            moved[2, rows, columns(t)] = (rate_minus * edge).astype(BF16)
            moved[3, rows, columns(t)] = (rate_plus * edge).astype(BF16)

    squared = first * first
    for p in range(planes):
        kept = alone_ref[p]
        if p in (0, planes - 1):
            arrived = squared[p : p + 1] * mix(matrix, moved[min(p, 1)])
            kept = (kept.astype(F32) + arrived).astype(BF16)
        held[p + 1] = kept
        out_ref[p] = kept
    held[0] = (beyond[0:1] * beyond[0:1] * mix(matrix, moved[2])).astype(BF16)
    held[planes + 1] = (beyond[2:3] * beyond[2:3] * mix(matrix, moved[3])).astype(BF16)
    count = planes + 2

    @pl.loop(0, orient // ROWS)
    def _(index):
        rows = rows_of(index)
        geo = geometry(v_ref, rows)
        _, rate_plus, rate_minus = face_parts(v_ref, rows)
        loaded = [load_plane(held, p, rows) for p in range(count)]
        for p in range(count):
            before = loaded[p - 1] if p > 0 else None
            after = loaded[p + 1] if p < count - 1 else None
            store_plane(moved, p + 1, rows, drift(loaded[p], before, after, geo))
        store_plane(moved, 0, rows, [rate_minus * tile for tile in loaded[0]])
        store_plane(moved, count + 1, rows, [rate_plus * tile for tile in loaded[-1]])

    cross = first * second
    factors = [beyond[1:2] * beyond[5:6], beyond[0:1] * beyond[4:5]]
    factors += [cross[p : p + 1] for p in range(planes)]
    factors += [beyond[2:3] * beyond[6:7], beyond[3:4] * beyond[7:8]]
    for p, factor in enumerate(factors):
        next_ref[p] = (factor * mix(matrix, moved[p])).astype(BF16)


def third_step_kernel(
    held_ref, mine_ref, other_ref, first_ref, second_ref, beyond_ref, v_ref, m_ref, out_ref, next_ref, held, moved
):
    planes, orient, _ = out_ref.shape
    matrix = m_ref[...]
    first, second = boltzmann(first_ref[...]), boltzmann(second_ref[...])
    beyond = boltzmann(beyond_ref[...])
    face_drifts(v_ref, mine_ref, other_ref, moved, (0, 1))
    cross = first * second
    for p in range(planes):
        kept = held_ref[p + 2]
        if p in (0, planes - 1):
            arrived = cross[p : p + 1] * mix(matrix, moved[min(p, 1)])
            kept = (kept.astype(F32) + arrived).astype(BF16)
        held[p] = kept
        out_ref[p] = kept

    @pl.loop(0, orient // ROWS)
    def _(index):
        rows = rows_of(index)
        geo = geometry(v_ref, rows)
        loaded = [load_plane(held_ref, p, rows) for p in (0, 1)]
        loaded += [load_plane(held, p, rows) for p in range(planes)]
        loaded += [load_plane(held_ref, p, rows) for p in (planes + 2, planes + 3)]
        for p in range(planes + 2):
            store_plane(moved, p, rows, drift(loaded[p + 1], loaded[p], loaded[p + 2], geo))

    squared = second * second
    factors = [beyond[4:5] * beyond[4:5]] + [squared[p : p + 1] for p in range(planes)] + [beyond[6:7] * beyond[6:7]]
    for p, factor in enumerate(factors):
        next_ref[p] = (factor * mix(matrix, moved[p])).astype(BF16)


def pairing_kernel(
    held_ref, mine_ref, other_ref, second_ref, v_ref, m_ref, weight_ref, partner_ref, out_ref, held, moved
):
    planes, orient, cells = partner_ref.shape
    second = boltzmann(second_ref[...])
    squared = second * second
    face_drifts(v_ref, mine_ref, other_ref, moved, (0, 1))
    for p in range(planes):
        kept = held_ref[p + 1]
        if p in (0, planes - 1):
            arrived = squared[p : p + 1] * mix(m_ref[...], moved[min(p, 1)])
            kept = (kept.astype(F32) + arrived).astype(BF16)
        held[p] = kept

    tiles = cells // LANES

    def fold(value):
        return jnp.sum(value.reshape(ROWS // 8, 8, LANES), axis=0)

    def body(index, sums):
        rows = rows_of(index)
        geo = geometry(v_ref, rows)
        loaded = [load_plane(held_ref, 0, rows)]
        loaded += [load_plane(held, p, rows) for p in range(planes)]
        loaded += [load_plane(held_ref, planes + 1, rows)]
        new = []
        for p in range(planes):
            moved_tiles = drift(loaded[p + 1], loaded[p], loaded[p + 2], geo)
            weights = load_plane(weight_ref, p, rows)
            partner = load_plane(partner_ref, p, rows)
            for t in range(tiles):
                last, third = sums[2 * (p * tiles + t)], sums[2 * (p * tiles + t) + 1]
                new.append(last + fold(moved_tiles[t] * weights[t]))
                new.append(third + fold(loaded[p + 1][t] * partner[t]))
        return tuple(new)

    zero = jnp.zeros((8, LANES), F32)
    sums = lax.fori_loop(0, orient // ROWS, body, (zero,) * (2 * planes * tiles))
    for p in range(planes):
        for t in range(tiles):
            last = jnp.sum(sums[2 * (p * tiles + t)], axis=0, keepdims=True)
            third = jnp.sum(sums[2 * (p * tiles + t) + 1], axis=0, keepdims=True)
            factor = second[p : p + 1, columns(t)]
            out_ref[p : p + 1, columns(t)] = (0.5 * factor * last + third / (factor * factor)) / orient


def kernel_call(kernel, outs, scratch, args):
    vmem = pl.BlockSpec(memory_space=pltpu.VMEM)
    return pl.pallas_call(
        kernel,
        out_shape=outs,
        in_specs=[vmem] * len(args),
        out_specs=jax.tree.map(lambda _: vmem, outs),
        scratch_shapes=[pltpu.VMEM(shape, BF16) for shape in scratch],
        compiler_params=pltpu.CompilerParams(vmem_limit_bytes=24 << 20),
    )(*args)


def shards(fields, end_weights, directions, analysis, synthesis, decay_rates):
    device = lax.axis_index("space")
    core = device % 2
    is_first = core == 0
    planes, cells = fields.shape
    orient = end_weights.shape[0]
    plane_index = device // 2 * planes + lax.broadcasted_iota(jnp.int32, (planes, 1), 0)
    ramp = slope * plane_index.astype(F32) / (planes * lax.axis_size("space") // 2)
    own = fields + ramp
    partner = swap_species(fields) + ramp

    velocity = jnp.where(is_first, 1.0, -1.0) * directions
    ahead = (directions[0] > 0)[:, None]
    plus_x = (velocity[0] > 0)[:, None]
    spread = jnp.concatenate([velocity, directions[:1]])[:, :, None]
    spread = jnp.broadcast_to(spread, (4, orient, LANES))

    def message(mine, other):
        return jnp.where(ahead, mine, other)

    faces = jnp.where(plus_x, boltzmann(own[-1]) * end_weights[:, -1].astype(F32), boltzmann(own[0]) * end_weights[:, 0].astype(F32))
    edge0 = faces.astype(BF16)
    near = jnp.where(is_first, jnp.stack([own[-1], own[-2]]), own[:2])
    near_other = jnp.where(is_first, jnp.stack([partner[-1], partner[-2]]), partner[:2])
    field_rows = jnp.concatenate([near, near_other])
    high = lax.reduce_precision(field_rows, 8, 7)
    coded = jnp.concatenate([high, field_rows - high, jnp.zeros((8, cells), F32)]).astype(BF16)
    arrived0 = to_next_slab(jnp.concatenate([message(edge0, swap_species(edge0)), coded]))
    crossed0 = swap_species(arrived0)

    scaled = synthesis.astype(F32) * decay_rates[None]
    mixing = jnp.dot(scaled, analysis.astype(F32), precision=lax.Precision.HIGHEST) + 1.0 / orient
    matrix = mixing.astype(BF16)

    start = jnp.transpose(end_weights, (1, 0, 2))
    slab = jax.ShapeDtypeStruct((planes, orient, cells), BF16)
    wide = lambda extra: jax.ShapeDtypeStruct((planes + extra, orient, cells), BF16)
    alone, edges = kernel_call(
        alone_kernel,
        (slab, jax.ShapeDtypeStruct((STEPS - 1, orient, cells), BF16)),
        (slab.shape, slab.shape),
        (start, own, partner, spread, matrix),
    )
    swapped_edges = swap_species(edges)
    arrived = [to_next_slab(message(edges[s], swapped_edges[s])) for s in range(STEPS - 1)]
    crossed = [swap_species(block) for block in arrived[:-1]]

    def near_fields(block):
        rows = block[orient : orient + 4].astype(F32) + block[orient + 4 : orient + 8].astype(F32)
        return rows[:2], rows[2:]

    mine_first, mine_second = near_fields(arrived0)
    other_second, other_first = near_fields(crossed0)
    low_first = jnp.where(is_first, mine_first, other_first)
    high_first = jnp.where(is_first, other_first, mine_first)
    low_second = jnp.where(is_first, mine_second, other_second)
    high_second = jnp.where(is_first, other_second, mine_second)
    beyond = jnp.concatenate([low_first, high_first, low_second, high_second])

    first_state, second_state = kernel_call(
        second_step_kernel,
        (slab, wide(4)),
        (wide(2).shape, wide(4).shape),
        (alone, edge0, arrived0[:orient], crossed0[:orient], own, partner, beyond, spread, matrix),
    )
    middle, third_state = kernel_call(
        third_step_kernel,
        (slab, wide(2)),
        (slab.shape, wide(2).shape),
        (second_state, arrived[0], crossed[0], own, partner, beyond, spread, matrix),
    )

    half = planes // 2
    sent_middle = jnp.where(is_first, middle[half:], middle[:half])
    kept_middle = jnp.where(is_first, middle[:half], middle[half:])
    met = jnp.sum(kept_middle.astype(F32) * swap_species(sent_middle).astype(F32), axis=1) / orient
    own_half = lax.dynamic_slice_in_dim(own, core * half, half, 0)
    partner_half = lax.dynamic_slice_in_dim(partner, core * half, half, 0)
    met = met / (boltzmann(own_half) * boltzmann(partner_half))
    count = lax.axis_size("space")
    sums = lax.all_to_all(jnp.broadcast_to(jnp.sum(met), (count, 1, LANES)), "space", 0, 0)
    partition = jnp.sum(sums[:, 0, 0]) / (count // 2 * planes * cells)
    met = lax.dynamic_update_slice_in_dim(jnp.zeros((planes, cells), F32), 0.5 * met, core * half, 0)

    partner_start = swap_species(start)
    weights = jnp.einsum("vu,vpc->puc", matrix, jnp.transpose(partner_start, (1, 0, 2)), preferred_element_type=F32)
    face = core * (planes - 1)
    own_face = lax.dynamic_index_in_dim(start, face, 0, False)
    own_weight = jnp.einsum("vu,vc->uc", matrix, own_face, preferred_element_type=F32)
    partner_weight = lax.dynamic_index_in_dim(weights, face, 0, False)
    rate_x = (courant * jnp.abs(directions[0]))[:, None]
    last_weight = rate_x * jnp.where(ahead, partner_weight, own_weight)

    shared = kernel_call(
        pairing_kernel,
        jax.ShapeDtypeStruct((planes, cells), F32),
        (slab.shape, (2, orient, cells)),
        (third_state, arrived[1], crossed[1], partner, spread, matrix, weights.astype(BF16), swap_species(first_state)),
    )
    product = last_weight * arrived[2].astype(F32)
    sent_face = 0.5 * jnp.sum(jnp.where(ahead, product, 0.0), axis=0) / orient
    kept_face = 0.5 * jnp.sum(jnp.where(ahead, 0.0, product), axis=0) / orient
    on_face = lax.broadcasted_iota(jnp.int32, (planes, 1), 0) == face
    sent = shared + met + jnp.where(on_face, boltzmann(partner) * sent_face, 0.0)
    kept = met + jnp.where(on_face, boltzmann(own) * kept_face, 0.0)
    return (kept + swap_species(sent)) / partition


def solution(mesh):
    return jax.shard_map(
        shards,
        mesh=mesh,
        in_specs=(P(("runs", "space"), None), P(None, ("runs", "space"), None), P(), P(), P(), P()),
        out_specs=P(("runs", "space"), None),
        check_vma=False,
    )
```

time: 134 us -> 66.9 us (0.50)
  blocking collectives: 31.1 us -> 0 us
  other arithmetic: 26.2 us -> 3.55 us
  Pallas kernels: 0 us -> 17.4 us
  local copies, waits for them, and re-layouts: 14.7 us -> 2.97 us
  matrix products: 8.01 us -> 0.97 us
  waiting for transfers between devices: 29.2 us -> 23.3 us
  starting transfers between devices: 23 us -> 17.5 us
    psum x1 -> x0, blocking collectives: 31.1 us -> none  [partition_of(): return lax.psum(local_total, 'space') / cell_count]
    reduce_sum x8 -> x4, other arithmetic: 25 us -> 1.7 us  [the longest x1 0.64 us: shards(): jnp.sum(met)]
    pallas_call x0 -> x4, Pallas kernels: none -> 17.4 us  [kernel_call(): pl.pallas_call(kernel, out_shape=outs, in_specs=[vmem] * len(args), out_s...]
    ppermute x19 -> x14, starting transfers between devices: 23 us -> 10.6 us  [the longest x4 7.5 us: to_next_slab(): lax.ppermute(block, 'space', [(i, (i + (2 if i % 2 == 0 else -2)) % count...]
    slice x32 -> x3, local copies, waits for them, and re-layouts: 12.4 us -> 0.04 us  [the longest x1 0.02 us: shards(): arrived0[:orient]]
    ppermute x19 -> x14, waiting for transfers between devices: 29.2 us -> 21.2 us  [the longest x4 18.2 us: to_next_slab(): lax.ppermute(block, 'space', [(i, (i + (2 if i % 2 == 0 else -2)) % count...]
    dot_general x4 -> x3, matrix products: 8.01 us -> 0.97 us  [the longest x1 0.45 us: shards(): jnp.einsum('vu,vpc->puc', matrix, jnp.transpose(partner_start, (1, 0, 2))...]
    all_to_all x0 -> x1, starting transfers between devices: none -> 6.89 us  [shards(): lax.all_to_all(jnp.broadcast_to(jnp.sum(met), (count, 1, LANES)), 'space'...]
  transfers between devices with their start and end apart: 19 -> 15, of which waited for: 14 -> 5; matrix products, arithmetic and copies ran while one was open for 3% -> 10% of each run, Pallas kernels for 0% -> 26%
where the time goes in v1:
time: 66.9 us; the launch traced here: 66.7 us
  waiting for transfers between devices  23.3 us (35%)
  starting transfers between devices  17.5 us (26%)
  Pallas kernels  17.4 us (26%)
  other arithmetic  3.55 us (5%)
  local copies, waits for them, and re-layouts  2.97 us (4%)
  matrix products  0.97 us (1%)
  between operations  0.97 us (1%)
    ppermute x4, waiting for transfers between devices, to_next_slab(): lax.ppermute(block, 'space', [(i, (i + (2 if i % 2 == 0 else -2)) % count...  18.2 us
    pallas_call x4, Pallas kernels, kernel_call(): pl.pallas_call(kernel, out_shape=outs, in_specs=[vmem] * len(args), out_s...  17.4 us
    ppermute x4, starting transfers between devices, to_next_slab(): lax.ppermute(block, 'space', [(i, (i + (2 if i % 2 == 0 else -2)) % count...  7.5 us
    all_to_all x1, starting transfers between devices, shards(): lax.all_to_all(jnp.broadcast_to(jnp.sum(met), (count, 1, LANES)), 'space'...  6.89 us
    ppermute x10, starting transfers between devices, swap_species(): return lax.ppermute(block, 'space', [(i ^ 1, i) for i in range(count)])  3.15 us
    ppermute x10, waiting for transfers between devices, swap_species(): return lax.ppermute(block, 'space', [(i ^ 1, i) for i in range(count)])  2.95 us
    all_to_all x1, waiting for transfers between devices, shards(): lax.all_to_all(jnp.broadcast_to(jnp.sum(met), (count, 1, LANES)), 'space'...  2.1 us
    unnamed x11, local copies, waits for them, and re-layouts  1.44 us
  transfers between devices with their start and end apart: 15, of which 5 were waited for; matrix products, arithmetic and copies ran while one was open for 10% of the time, Pallas kernels for 26%

profile of v1, /device:TPU:0, one launch (start us, length us, event | category | flops | bytes accessed | tf_op | source)
XLA Modules:
  0.0 66.7 jit_solution(15439566690537048794)
XLA Ops:
  0.0 0.5 collective-permute-start.1
  0.5 1.4 %copy.26 = bf16[256,4,512]{2,0,1:T(8,128)(2,1)S(1)} copy(bf16[256,4,512]{2,1,0:T(4,128)(2,1)} %param.7) | data formatting | bytes 2097152 | tf_op args[1]
  2.3 0.3 fusion.m_ref
  2.6 0.2 fusion.10
  3.0 0.2 broadcast_in_dim.86.v_ref
  3.2 6.0 %shard_map.64 = (bf16[4,256,512]{2,1,0:T(8,128)(2,1)S(1)}, bf16[3,256,512]{2,1,0:T(8,128)(2,1)S(1)}) custom-call(bf16[4,256,512]{2,1,0:T(8,128)(2,1)S(1)} %bitcast.58, f32[4,512]{1,0:T(4,128)S(1)} %get-tuple-element.44.first_ref, f32[4,512]{1,0:T(4,128)S(1)} %get-tuple-element.43.second_ref, f32[4,256,128]{2,1,0:T(8,128)S(1)} %broadcast_in_dim.86.v_ref, ...), custom_call_target="tpu_custom_call" | custom-call | tf_op jit(solution)/shard_map/pallas_call | solution.py:284
  9.2 0.5 collective-permute-start.2
  10.0 1.9 %collective-permute-done.4 = bf16[256,512]{1,0:T(8,128)(2,1)S(1)} collective-permute-done((bf16[256,512]{1,0:T(8,128)(2,1)S(1)}, bf16[256,512]{1,0:T(8,128)(2,1)S(1)}, u32[]{:S(2)}, u32[]{:S(2)}) %collective-permute-start.4) | collective-permute-done | bytes 262176 | tf_op jit(solution)/shard_map/ppermute | solution.py:24
  12.0 0.4 fusion.7
  12.5 2.9 %collective-permute-start.5 = (bf16[272,512]{1,0:T(8,128)(2,1)S(1)}, bf16[272,512]{1,0:T(8,128)(2,1)S(1)}, u32[]{:S(2)}, u32[]{:S(2)}) collective-permute-start(bf16[272,512]{1,0:T(8,128)(2,1)S(1)} %maximum_maximum_fusion), channel_id=1, source_target_pairs={{0,2},{1,15},{2,4},{3,1},{4,6},{5,3},{6,8},{7,5},{8,10},{9,7},{10,... | collective-permute-start | bytes 835592 | tf_op jit(solution)/shard_map/ppermute | solution.py:29
  15.4 1.5 %collective-permute-start.7 = (bf16[256,512]{1,0:T(8,128)(2,1)S(1)}, bf16[256,512]{1,0:T(8,128)(2,1)S(1)}, u32[]{:S(2)}, u32[]{:S(2)}) collective-permute-start(bf16[256,512]{1,0:T(8,128)(2,1)S(1)} %get-tuple-element.22), channel_id=1, source_target_pairs={{0,2},{1,15},{2,4},{3,1},{4,6},{5,3},{6,8},{7,5},{8,10},{9,7},{10,... | collective-permute-start | bytes 786440 | tf_op jit(solution)/shard_map/ppermute | solution.py:29
  16.9 1.5 %collective-permute-start.10 = (bf16[256,512]{1,0:T(8,128)(2,1)S(1)}, bf16[256,512]{1,0:T(8,128)(2,1)}, u32[]{:S(2)}, u32[]{:S(2)}) collective-permute-start(bf16[256,512]{1,0:T(8,128)(2,1)S(1)} %get-tuple-element.21), channel_id=1, source_target_pairs={{0,2},{1,15},{2,4},{3,1},{4,6},{5,3},{6,8},{7,5},{8,10},{9,7},{10,... | collective-permute-start | bytes 786440 | tf_op jit(solution)/shard_map/ppermute | solution.py:29
  18.4 1.5 %collective-permute-start.3 = (bf16[256,512]{1,0:T(8,128)(2,1)S(1)}, bf16[256,512]{1,0:T(8,128)(2,1)S(1)}, u32[]{:S(2)}, u32[]{:S(2)}) collective-permute-start(bf16[256,512]{1,0:T(8,128)(2,1)S(1)} %get-tuple-element.23), channel_id=1, source_target_pairs={{0,2},{1,15},{2,4},{3,1},{4,6},{5,3},{6,8},{7,5},{8,10},{9,7},{10,... | collective-permute-start | bytes 786440 | tf_op jit(solution)/shard_map/ppermute | solution.py:29
  20.0 0.5 fusion.1
  20.6 13.1 %collective-permute-done.7.mine_ref = bf16[256,512]{1,0:T(8,128)(2,1)S(1)} collective-permute-done((bf16[256,512]{1,0:T(8,128)(2,1)S(1)}, bf16[256,512]{1,0:T(8,128)(2,1)S(1)}, u32[]{:S(2)}, u32[]{:S(2)}) %collective-permute-start.7) | collective-permute-done | bytes 262176 | tf_op jit(solution)/shard_map/ppermute | solution.py:29
  33.7 0.3 collective-permute-start.8
  34.2 5.1 %collective-permute-done.3 = bf16[256,512]{1,0:T(8,128)(2,1)S(1)} collective-permute-done((bf16[256,512]{1,0:T(8,128)(2,1)S(1)}, bf16[256,512]{1,0:T(8,128)(2,1)S(1)}, u32[]{:S(2)}, u32[]{:S(2)}) %collective-permute-start.3) | collective-permute-done | bytes 262176 | tf_op jit(solution)/shard_map/ppermute | solution.py:29
  39.3 0.2 select_reduce_fusion
  39.7 4.2 %shard_map.65 = (bf16[4,256,512]{2,1,0:T(8,128)(2,1)}, bf16[8,256,512]{2,1,0:T(8,128)(2,1)S(1)}) custom-call(bf16[4,256,512]{2,1,0:T(8,128)(2,1)S(1)} %get-tuple-element.12.alone_ref, bf16[256,512]{1,0:T(8,128)(2,1)S(1)} %fusion.4.edge_ref, bf16[256,512]{1,0:T(8,128)(2,1)S(1)} %slice.136.mine_ref, bf16[256,512]{1,0:T(8,128)(2,1)S(1)} %slice.137.other_ref, ...), custom_call_target="tpu_custom_call" | custom-call | tf_op jit(solution)/shard_map/pallas_call | solution.py:284
  43.9 3.5 %shard_map.66 = (bf16[4,256,512]{2,1,0:T(8,128)(2,1)S(1)}, bf16[6,256,512]{2,1,0:T(8,128)(2,1)S(1)}) custom-call(bf16[8,256,512]{2,1,0:T(8,128)(2,1)S(1)} %get-tuple-element.13.held_ref, bf16[256,512]{1,0:T(8,128)(2,1)S(1)} %collective-permute-done.7.mine_ref, bf16[256,512]{1,0:T(8,128)(2,1)S(1)} %collective-permute-done.8.other_ref, ...), custom_call_target="tpu_custom_call" | custom-call | tf_op jit(solution)/shard_map/pallas_call | solution.py:284
  47.5 0.4 collective-permute-start.9
  48.1 0.3 collective-permute-start.11
  48.5 1.0 %collective-permute-done.9 = bf16[2,256,512]{2,1,0:T(8,128)(2,1)S(1)} collective-permute-done((bf16[2,256,512]{2,1,0:T(8,128)(2,1)S(1)}, bf16[2,256,512]{2,1,0:T(8,128)(2,1)S(1)}, u32[]{:S(2)}, u32[]{:S(2)}) %collective-permute-start.9) | collective-permute-done | bytes 524320 | tf_op jit(solution)/shard_map/ppermute | solution.py:24
  49.5 0.2 multiply_reduce_fusion
  49.7 0.6 fusion.20
  50.4 1.2 %broadcast_in_dim.90 = f32[16,1,128]{2,1,0:T(1,128)} broadcast(f32[]{:T(128)} %get-tuple-element.19), dimensions={} | broadcast | bytes 8196 | tf_op jit(solution)/shard_map/broadcast_in_dim | solution.py:374
  51.6 6.9 %all-to-all-start = ((f32[16,1,128]{2,1,0:T(1,128)}), f32[16,1,128]{2,1,0:T(1,128)S(1)}, u32[]{:S(2)}, u32[]{:S(2)}) async-start(f32[16,1,128]{2,1,0:T(1,128)} %broadcast_in_dim.90), calls=%async_computation | async-start | bytes 16384 | tf_op jit(solution)/shard_map/all_to_all | solution.py:374
  58.5 3.7 %shard_map.67 = f32[4,512]{1,0:T(4,128)S(1)} custom-call(bf16[6,256,512]{2,1,0:T(8,128)(2,1)S(1)} %get-tuple-element.15.held_ref, bf16[256,512]{1,0:T(8,128)(2,1)} %collective-permute-done.10.mine_ref, bf16[256,512]{1,0:T(8,128)(2,1)} %collective-permute-done.11.other_ref, f32[4,512]{1,0:T(4,128)S(1)} %get-tuple-element.43.second_ref, ...), custom_call_target="tpu_custom_call" | custom-call | tf_op jit(solution)/shard_map/pallas_call | solution.py:284
  62.3 0.4 collective-permute-start.13
  62.7 2.1 %all-to-all-done = f32[16,1,128]{2,1,0:T(1,128)S(1)} async-done(((f32[16,1,128]{2,1,0:T(1,128)}), f32[16,1,128]{2,1,0:T(1,128)S(1)}, u32[]{:S(2)}, u32[]{:S(2)}) %all-to-all-start) | async-done | bytes 8224 | tf_op jit(solution)/shard_map/all_to_all | solution.py:374
  64.8 0.6 slice_reduce_fusion
  66.1 0.6 add_divide_fusion
  (53 shorter events, 1.7 us)
Async XLA Ops:
  0.0 2.2 %copy-start = (bf16[256,256]{1,0:T(8,128)(2,1)S(1)}, bf16[256,256]{1,0:T(8,128)(2,1)}, u32[]{:S(2)}) copy-start(bf16[256,256]{1,0:T(8,128)(2,1)} %param.9) | copy-start | bytes 393220
  0.0 2.9 %copy-start.2 = (f32[4,512]{1,0:T(4,128)S(1)}, f32[4,512]{1,0:T(4,128)}, u32[]{:S(2)}) copy-start(f32[4,512]{1,0:T(4,128)} %param.6) | copy-start | bytes 24580
  0.0 2.1 %copy-start.3 = (f32[3,256]{1,0:T(4,128)S(1)}, f32[3,256]{1,0:T(4,128)}, u32[]{:S(2)}) copy-start(f32[3,256]{1,0:T(4,128)} %param.8) | copy-start | bytes 9220
  0.0 2.2 %copy-start.1 = (bf16[256,256]{1,0:T(8,128)(2,1)S(1)}, bf16[256,256]{1,0:T(8,128)(2,1)}, u32[]{:S(2)}) copy-start(bf16[256,256]{1,0:T(8,128)(2,1)} %param.10) | copy-start | bytes 393220
  0.0 2.3 %copy-start.4 = (f32[256]{0:T(256)S(1)}, f32[256]{0:T(256)}, u32[]{:S(2)}) copy-start(f32[256]{0:T(256)} %param.11) | copy-start | bytes 3076
  0.0 2.9 %collective-permute-start.1 = (f32[4,512]{1,0:T(4,128)}, f32[4,512]{1,0:T(4,128)S(1)}, u32[]{:S(2)}, u32[]{:S(2)}) collective-permute-start(f32[4,512]{1,0:T(4,128)} %param.6), channel_id=1, source_target_pairs={{1,0},{0,1},{3,2},{2,3},{5,4},{4,5},{7,6},{6,7},{9,8},{8,9},{11,10... | collective-permute-start | bytes 24584 | tf_op jit(solution)/shard_map/ppermute | solution.py:24
  2.0 18.0 %collective-permute-start = (bf16[4,256,512]{2,1,0:T(8,128)(2,1)S(1)}, bf16[4,256,512]{2,1,0:T(8,128)(2,1)S(1)}, u32[]{:S(2)}, u32[]{:S(2)}) collective-permute-start(bf16[4,256,512]{2,1,0:T(8,128)(2,1)S(1)} %bitcast.57), channel_id=1, source_target_pairs={{1,0},{0,1},{3,2},{2,3},{5,4},{4,5},{7,6},{6,7},{9,8},{8,9},{11,10... | collective-permute-start | bytes 3145736 | tf_op jit(solution)/shard_map/ppermute | solution.py:24
  9.2 2.8 %collective-permute-start.2 = (bf16[3,256,512]{2,1,0:T(8,128)(2,1)S(1)}, bf16[3,256,512]{2,1,0:T(8,128)(2,1)S(1)}, u32[]{:S(2)}, u32[]{:S(2)}) collective-permute-start(bf16[3,256,512]{2,1,0:T(8,128)(2,1)S(1)} %get-tuple-element.11), channel_id=1, source_target_pairs={{1,0},{0,1},{3,2},{2,3},{5,4},{4,5},{7,6},{6,7},{9,8},{8,9},{11,10... | collective-permute-start | bytes 2359304 | tf_op jit(solution)/shard_map/ppermute | solution.py:24
  9.8 2.1 %collective-permute-start.4 = (bf16[256,512]{1,0:T(8,128)(2,1)S(1)}, bf16[256,512]{1,0:T(8,128)(2,1)S(1)}, u32[]{:S(2)}, u32[]{:S(2)}) collective-permute-start(bf16[256,512]{1,0:T(8,128)(2,1)S(1)} %fusion.4.edge_ref), channel_id=1, source_target_pairs={{1,0},{0,1},{3,2},{2,3},{5,4},{4,5},{7,6},{6,7},{9,8},{8,9},{11,10... | collective-permute-start | bytes 786440 | tf_op jit(solution)/shard_map/ppermute | solution.py:24
  12.5 21.6 %collective-permute-start.5 = (bf16[272,512]{1,0:T(8,128)(2,1)S(1)}, bf16[272,512]{1,0:T(8,128)(2,1)S(1)}, u32[]{:S(2)}, u32[]{:S(2)}) collective-permute-start(bf16[272,512]{1,0:T(8,128)(2,1)S(1)} %maximum_maximum_fusion), channel_id=1, source_target_pairs={{0,2},{1,15},{2,4},{3,1},{4,6},{5,3},{6,8},{7,5},{8,10},{9,7},{10,... | collective-permute-start | bytes 835592 | tf_op jit(solution)/shard_map/ppermute | solution.py:29
  15.4 18.3 %collective-permute-start.7 = (bf16[256,512]{1,0:T(8,128)(2,1)S(1)}, bf16[256,512]{1,0:T(8,128)(2,1)S(1)}, u32[]{:S(2)}, u32[]{:S(2)}) collective-permute-start(bf16[256,512]{1,0:T(8,128)(2,1)S(1)} %get-tuple-element.22), channel_id=1, source_target_pairs={{0,2},{1,15},{2,4},{3,1},{4,6},{5,3},{6,8},{7,5},{8,10},{9,7},{10,... | collective-permute-start | bytes 786440 | tf_op jit(solution)/shard_map/ppermute | solution.py:29
  16.9 31.2 %collective-permute-start.10 = (bf16[256,512]{1,0:T(8,128)(2,1)S(1)}, bf16[256,512]{1,0:T(8,128)(2,1)}, u32[]{:S(2)}, u32[]{:S(2)}) collective-permute-start(bf16[256,512]{1,0:T(8,128)(2,1)S(1)} %get-tuple-element.21), channel_id=1, source_target_pairs={{0,2},{1,15},{2,4},{3,1},{4,6},{5,3},{6,8},{7,5},{8,10},{9,7},{10,... | collective-permute-start | bytes 786440 | tf_op jit(solution)/shard_map/ppermute | solution.py:29
  18.4 20.9 %collective-permute-start.3 = (bf16[256,512]{1,0:T(8,128)(2,1)S(1)}, bf16[256,512]{1,0:T(8,128)(2,1)S(1)}, u32[]{:S(2)}, u32[]{:S(2)}) collective-permute-start(bf16[256,512]{1,0:T(8,128)(2,1)S(1)} %get-tuple-element.23), channel_id=1, source_target_pairs={{0,2},{1,15},{2,4},{3,1},{4,6},{5,3},{6,8},{7,5},{8,10},{9,7},{10,... | collective-permute-start | bytes 786440 | tf_op jit(solution)/shard_map/ppermute | solution.py:29
  33.7 10.2 %collective-permute-start.8 = (bf16[256,512]{1,0:T(8,128)(2,1)S(1)}, bf16[256,512]{1,0:T(8,128)(2,1)S(1)}, u32[]{:S(2)}, u32[]{:S(2)}) collective-permute-start(bf16[256,512]{1,0:T(8,128)(2,1)S(1)} %collective-permute-done.7.mine_ref), channel_id=1, source_target_pairs={{1,0},{0,1},{3,2},{2,3},{5,4},{4,5},{7,6},{6,7},{9,8},{8,9},{11,10... | collective-permute-start | bytes 786440 | tf_op jit(solution)/shard_map/ppermute | solution.py:24
  34.0 5.6 %collective-permute-start.6 = (bf16[272,512]{1,0:T(8,128)(2,1)S(1)}, bf16[272,512]{1,0:T(8,128)(2,1)S(1)}, u32[]{:S(2)}, u32[]{:S(2)}) collective-permute-start(bf16[272,512]{1,0:T(8,128)(2,1)S(1)} %collective-permute-done.5), channel_id=1, source_target_pairs={{1,0},{0,1},{3,2},{2,3},{5,4},{4,5},{7,6},{6,7},{9,8},{8,9},{11,10... | collective-permute-start | bytes 835592 | tf_op jit(solution)/shard_map/ppermute | solution.py:24
  47.5 2.0 %collective-permute-start.9 = (bf16[2,256,512]{2,1,0:T(8,128)(2,1)S(1)}, bf16[2,256,512]{2,1,0:T(8,128)(2,1)S(1)}, u32[]{:S(2)}, u32[]{:S(2)}) collective-permute-start(bf16[2,256,512]{2,1,0:T(8,128)(2,1)S(1)} %broadcast_select_fusion), channel_id=1, source_target_pairs={{1,0},{0,1},{3,2},{2,3},{5,4},{4,5},{7,6},{6,7},{9,8},{8,9},{11,10... | collective-permute-start | bytes 1572872 | tf_op jit(solution)/shard_map/ppermute | solution.py:24
  47.9 10.6 %collective-permute-start.12 = (bf16[4,256,512]{2,1,0:T(8,128)(2,1)}, bf16[4,256,512]{2,1,0:T(8,128)(2,1)}, u32[]{:S(2)}, u32[]{:S(2)}) collective-permute-start(bf16[4,256,512]{2,1,0:T(8,128)(2,1)} %get-tuple-element.16), channel_id=1, source_target_pairs={{1,0},{0,1},{3,2},{2,3},{5,4},{4,5},{7,6},{6,7},{9,8},{8,9},{11,10... | collective-permute-start | bytes 3145736 | tf_op jit(solution)/shard_map/ppermute | solution.py:24
  48.1 10.4 %collective-permute-start.11 = (bf16[256,512]{1,0:T(8,128)(2,1)}, bf16[256,512]{1,0:T(8,128)(2,1)}, u32[]{:S(2)}, u32[]{:S(2)}) collective-permute-start(bf16[256,512]{1,0:T(8,128)(2,1)} %collective-permute-done.10.mine_ref), channel_id=1, source_target_pairs={{1,0},{0,1},{3,2},{2,3},{5,4},{4,5},{7,6},{6,7},{9,8},{8,9},{11,10... | collective-permute-start | bytes 786440 | tf_op jit(solution)/shard_map/ppermute | solution.py:24
  51.6 13.2 %all-to-all-start = ((f32[16,1,128]{2,1,0:T(1,128)}), f32[16,1,128]{2,1,0:T(1,128)S(1)}, u32[]{:S(2)}, u32[]{:S(2)}) async-start(f32[16,1,128]{2,1,0:T(1,128)} %broadcast_in_dim.90), calls=%async_computation | async-start | bytes 16384 | tf_op jit(solution)/shard_map/all_to_all | solution.py:374
  62.3 3.8 %collective-permute-start.13 = (f32[4,512]{1,0:T(4,128)S(1)}, f32[4,512]{1,0:T(4,128)S(1)}, u32[]{:S(2)}, u32[]{:S(2)}) collective-permute-start(f32[4,512]{1,0:T(4,128)S(1)} %select_add_fusion), channel_id=1, source_target_pairs={{1,0},{0,1},{3,2},{2,3},{5,4},{4,5},{7,6},{6,7},{9,8},{8,9},{11,10... | collective-permute-start | bytes 24584 | tf_op jit(solution)/shard_map/ppermute | solution.py:24
